TPU v7x, 32 devices: a whole 2x2x4 slice. The times are simulated.
32 devices in a mesh: row: 8 (over y, x, core), col: 4 (over z).
Axes of the slice: x: 2, y: 2, z: 4, core: 2. Of those that a mesh axis runs over, the one named last changes fastest.
Arguments:
- amplitudes: bfloat16 [64, 6400], P(('col', 'row')), may hold values from -6 to 6
- panel: bfloat16 [9600, 6400], P('col', 'row'), may hold values from -0.21875 to 0.21875
- irrep_ij: int32 [64], replicated, may hold values from 0 to 7
- irrep_ef: int32 [6400], replicated, may hold values from 0 to 7
Outputs:
- ladder: bfloat16 [64, 9600], P(('col', 'row'))
All inputs are finite; a program needn't handle non-finite values.
Results may differ from a plain program's by a relative error of at most 0.003.
Values may be sent and summed in bfloat16 or wider, within the bound.
A program may use at most 64 MiB of HBM per device.

v0:
```python
import jax
import jax.numpy as jnp
from jax import lax
from jax.sharding import PartitionSpec as P


def contract(left, right):
    return lax.dot_general(
        left, right, (((1,), (1,)), ((), ())), preferred_element_type=jnp.float32
    )


def ef_local(irrep_ij, irrep_ef, blocked):
    pair_rows = blocked.shape[0]
    pair_cols = blocked.shape[1]
    col_index = lax.axis_index("col")
    row_index = lax.axis_index("row")
    sym_rows = lax.dynamic_slice_in_dim(irrep_ij, col_index * pair_rows, pair_rows)
    sym_cols = lax.dynamic_slice_in_dim(irrep_ef, row_index * pair_cols, pair_cols)
    return jnp.where(sym_rows[:, None] == sym_cols[None, :], blocked, jnp.zeros_like(blocked))


def body(amplitudes, panel, irrep_ij, irrep_ef):
    blocked = lax.all_to_all(amplitudes, "row", split_axis=1, concat_axis=0, tiled=True)
    allowed = ef_local(irrep_ij, irrep_ef, blocked)
    partial_terms = contract(allowed, lax.all_gather(panel, "col", axis=0, tiled=True))
    summed = lax.psum_scatter(partial_terms, "row", scatter_dimension=0, tiled=True)
    return summed.astype(jnp.bfloat16)


def solution(mesh):
    in_specs = (P(("col", "row"), None), P("col", "row"), P(), P())
    out_specs = P(("col", "row"), None)
    return jax.shard_map(body, mesh=mesh, in_specs=in_specs, out_specs=out_specs, check_vma=False)
```

profile of v0, /device:TPU:0, one launch (start us, length us, event | category | flops | bytes accessed | tf_op | source)
XLA Modules:
  0.0 396.6 jit_solution(6917603864206018929)
XLA Ops:
  6.5 0.0 all-gather.3.cloned.1.call-start
  6.5 0.7 all-gather.3.cloned.1.call-update
  7.3 0.8 all_to_all.14
  8.1 0.6 copy.7
  8.7 5.2 %all-to-all-start = ((bf16[2,8,800]{2,0,1:T(2,128)(2,1)}), bf16[2,8,800]{2,0,1:T(2,128)(2,1)S(1)}, u32[]{:S(2)}, u32[]{:S(2)}) async-start(bf16[2,8,800]{2,0,1:T(2,128)(2,1)} %copy.7), calls=%async_computation | async-start | bytes 57344 | tf_op jit(solution)/shard_map/all_to_all | solution.py:24
  13.9 0.8 dynamic_slice.7
  14.7 0.7 dynamic_slice.6
  15.4 1.2 dynamic-slice
  17.2 1.5 all-to-all-done
  18.8 259.8 %all-gather.3.cloned.1.call-done = bf16[4,2400,800]{1,2,0:T(8,128)(2,1)} async-done(((bf16[1,2400,800]{1,2,0:T(8,128)(2,1)}), bf16[4,2400,800]{1,2,0:T(8,128)(2,1)}) %all-gather.3.cloned.1.call-update) | async-done | bytes 15360016 | tf_op jit(solution)/shard_map/all_gather | solution.py:26
  278.6 48.0 %copy.8 = bf16[4,2400,800]{1,0,2:T(4,128)(2,1)} copy(bf16[4,2400,800]{1,2,0:T(8,128)(2,1)} %all-gather.3.cloned.1.call-done) | data formatting | bytes 30720000 | tf_op jit(solution)/shard_map/all_gather | solution.py:26
  326.6 24.8 %reshape.6 = bf16[9600,800]{0,1:T(8,128)(2,1)} reshape(bf16[4,2400,800]{1,0,2:T(4,128)(2,1)} %copy.8) | data formatting | bytes 30720000
  351.5 6.6 %fusion = f32[16,9600]{1,0:T(8,128)S(1)} fusion(bf16[9600,800]{0,1:T(8,128)(2,1)} %reshape.6, bf16[16,800]{1,0:T(8,128)(2,1)S(1)} %all_to_all.17, s32[800]{0:T(1024)S(1)} %dynamic_slice.7, s32[16]{0:T(128)S(1)} %dynamic_slice.6), kind=kOutput, calls=%fused_computation.2 | convolution fusion | flops 245785600 | bytes 16003264 | tf_op jit(solution)/shard_map/dot_general | solution.py:8
  358.1 31.0 %all-reduce.2 = bf16[16,9600]{1,0:T(8,128)(2,1)S(1)} all-reduce(f32[16,9600]{1,0:T(8,128)S(1)} %fusion), channel_id=2, replica_groups=mesh['row'=8,'col'=4] {'row'}, use_global_device_ids=true, to_apply=%region_0.1.clone | all-reduce | flops 153600 | bytes 921600
  389.1 0.7 dynamic-slice_convert_fusion
  (1 shorter events, 0.0 us)
Async XLA Ops:
  6.5 272.1 %all-gather.3.cloned.1.call-start = ((), (), s32[]{:S(2)}) async-start(), calls=%async_computation.1 | async-start | bytes 19456000 | tf_op jit(solution)/shard_map/all_gather | solution.py:26
  8.7 10.0 %all-to-all-start = ((bf16[2,8,800]{2,0,1:T(2,128)(2,1)}), bf16[2,8,800]{2,0,1:T(2,128)(2,1)S(1)}, u32[]{:S(2)}, u32[]{:S(2)}) async-start(bf16[2,8,800]{2,0,1:T(2,128)(2,1)} %copy.7), calls=%async_computation | async-start | bytes 57344 | tf_op jit(solution)/shard_map/all_to_all | solution.py:24
Sparse Core Ops, SparseCore 0:
  8.9 269.6 all-gather.2
where the time goes:
time: 398 us; the launch traced here: 397 us
  waiting for transfers between devices  262 us (66%)
  local copies, waits for them, and re-layouts  77.8 us (20%)
  blocking collectives  31 us (8%)
  between operations  14 us (4%)
  matrix products  6.61 us (2%)
  starting transfers between devices  5.17 us (1%)
    all_gather x1, waiting for transfers between devices, body(): lax.all_gather(panel, 'col', axis=0, tiled=True)  260 us
    all_gather x1, local copies, waits for them, and re-layouts, body(): lax.all_gather(panel, 'col', axis=0, tiled=True)  48 us
    unnamed x1, blocking collectives  31 us
    unnamed x2, local copies, waits for them, and re-layouts  26.1 us
  transfers between devices with their start and end apart: 2, of which 2 were waited for; matrix products, arithmetic and copies ran while one was open for 1% of the time, Pallas kernels for 0%

commit v1 on v0

--- a/solution.py
+++ b/solution.py
@@ -2,6 +2,36 @@
 import jax.numpy as jnp
 from jax import lax
 from jax.sharding import PartitionSpec as P
+
+
+def spots_play(s0, dimension_no):
+    placed = list(s0.shape[1:])
+    placed[dimension_no] *= s0.shape[0]
+    lower = jnp.moveaxis(s0, 0, dimension_no).reshape(placed)
+    return lower
+
+
+def launch_regions_on(a0, bus_axis, row_dim):
+    wide_n = lax.axis_size(bus_axis)
+    top = range(wide_n)
+    m_next = map(lambda num: (num, (num + 1) % wide_n), top)
+    items = list(m_next)
+    runs = [(p, tick) for tick, p in items]
+    y2, last = ([], [])
+    for rr in range(wide_n - 1):
+        if rr % 2 == 0:
+            base_arr = lax.ppermute(y2[-1] if y2 else a0, bus_axis, items)
+            y2.append(base_arr)
+        else:
+            out_arr = lax.ppermute(last[-1] if last else a0, bus_axis, runs)
+            last.append(out_arr)
+    near = jnp.stack([*y2[::-1], a0, *last])
+    later = lax.axis_index(bus_axis)
+    carry = len(y2)
+    g_now = later - carry
+    near = near[(jnp.arange(wide_n) - g_now) % wide_n]
+    f_next = spots_play(near, row_dim)
+    return f_next
 
 
 def contract(left, right):
@@ -23,7 +53,7 @@
 def body(amplitudes, panel, irrep_ij, irrep_ef):
     blocked = lax.all_to_all(amplitudes, "row", split_axis=1, concat_axis=0, tiled=True)
     allowed = ef_local(irrep_ij, irrep_ef, blocked)
-    partial_terms = contract(allowed, lax.all_gather(panel, "col", axis=0, tiled=True))
+    partial_terms = contract(allowed, launch_regions_on(panel, bus_axis="col", row_dim=0))
     summed = lax.psum_scatter(partial_terms, "row", scatter_dimension=0, tiled=True)
     return summed.astype(jnp.bfloat16)
 

time: 398 us -> 397 us (level)
  other arithmetic: 0 us -> 38.7 us
  waiting for transfers between devices: 262 us -> 242 us
  between operations: 14 us -> 0.68 us
  local copies, waits for them, and re-layouts: 77.8 us -> 67.8 us
    all_gather x1 -> x0, waiting for transfers between devices: 260 us -> none  [body(): lax.all_gather(panel, 'col', axis=0, tiled=True)]
    ppermute x0 -> x3, waiting for transfers between devices: none -> 241 us  [the longest x2 169 us: launch_regions_on(): base_arr = lax.ppermute(y2[-1] if y2 else a0, bus_axis, items)]
    gather x0 -> x19, local copies, waits for them, and re-layouts: none -> 62.7 us
    all_gather x1 -> x0, local copies, waits for them, and re-layouts: 48 us -> none  [body(): lax.all_gather(panel, 'col', axis=0, tiled=True)]
    unnamed x2 -> x3, local copies, waits for them, and re-layouts: 26.1 us -> 1.27 us
    unnamed x0 -> x2, other arithmetic: none -> 19 us
    another operation x0 -> x1, other arithmetic: none -> 12.9 us  [launch_regions_on(): near = jnp.stack([*y2[::-1], a0, *last])]
    gather x0 -> x2, other arithmetic: none -> 6.72 us  [launch_regions_on(): near = near[(jnp.arange(wide_n) - g_now) % wide_n]]
  transfers between devices with their start and end apart: 2 -> 4, of which waited for: 2 -> 4; matrix products, arithmetic and copies ran while one was open for 1% -> 1% of each run, Pallas kernels for 0% -> 0%
where the time goes in v1:
time: 397 us; the launch traced here: 395 us
  waiting for transfers between devices  242 us (61%)
  local copies, waits for them, and re-layouts  67.8 us (17%)
  other arithmetic  38.7 us (10%)
  blocking collectives  28.9 us (7%)
  starting transfers between devices  9.02 us (2%)
  matrix products  8.26 us (2%)
    ppermute x2, waiting for transfers between devices, launch_regions_on(): base_arr = lax.ppermute(y2[-1] if y2 else a0, bus_axis, items)  169 us
    ppermute x1, waiting for transfers between devices, launch_regions_on(): out_arr = lax.ppermute(last[-1] if last else a0, bus_axis, runs)  71.7 us
    gather x16, local copies, waits for them, and re-layouts  37.1 us
    unnamed x1, blocking collectives  28.9 us
    gather x3, local copies, waits for them, and re-layouts, launch_regions_on(): near = near[(jnp.arange(wide_n) - g_now) % wide_n]  25.6 us
    unnamed x2, other arithmetic  19 us
    another operation x1, other arithmetic, launch_regions_on(): near = jnp.stack([*y2[::-1], a0, *last])  12.9 us
    dot_general x1, matrix products, contract(): lax.dot_general(left, right, (((1,), (1,)), ((), ())), preferred_element_...  8.26 us
  transfers between devices with their start and end apart: 4, of which 4 were waited for; matrix products, arithmetic and copies ran while one was open for 1% of the time, Pallas kernels for 0%

profile of v1, /device:TPU:0, one launch (start us, length us, event | category | flops | bytes accessed | tf_op | source)
XLA Modules:
  0.0 395.4 jit_solution(14728387603039528476)
XLA Ops:
  0.0 3.0 collective-permute-start
  3.0 2.0 collective-permute-start.2
  5.1 85.3 %collective-permute-done = bf16[2400,800]{0,1:T(8,128)(2,1)} collective-permute-done((bf16[2400,800]{0,1:T(8,128)(2,1)}, bf16[2400,800]{0,1:T(8,128)(2,1)}, u32[]{:S(2)}, u32[]{:S(2)}) %collective-permute-start) | collective-permute-done | bytes 3840032 | tf_op jit(solution)/shard_map/ppermute | solution.py:23
  90.3 0.0 collective-permute-start.1
  90.3 0.8 all_to_all.12
  91.2 0.6 copy.13
  91.8 4.0 %all-to-all-start = ((bf16[2,8,800]{2,0,1:T(2,128)(2,1)}), bf16[2,8,800]{2,0,1:T(2,128)(2,1)S(1)}, u32[]{:S(2)}, u32[]{:S(2)}) async-start(bf16[2,8,800]{2,0,1:T(2,128)(2,1)} %copy.13), calls=%async_computation | async-start | bytes 57344 | tf_op jit(solution)/shard_map/all_to_all | solution.py:54
  95.8 0.7 dynamic_slice.6
  96.6 0.1 eq.18
  96.7 0.8 dynamic_slice.7
  97.4 1.3 dynamic-slice.4
  99.3 1.3 all-to-all-done
  100.6 0.1 compare_select_fusion
  100.7 71.7 %collective-permute-done.2 = bf16[2400,800]{0,1:T(8,128)(2,1)} collective-permute-done((bf16[2400,800]{0,1:T(8,128)(2,1)}, bf16[2400,800]{0,1:T(8,128)(2,1)}, u32[]{:S(2)}, u32[]{:S(2)}) %collective-permute-start.2) | collective-permute-done | bytes 3840032 | tf_op jit(solution)/shard_map/ppermute | solution.py:26
  172.5 83.8 %collective-permute-done.1 = bf16[2400,800]{0,1:T(8,128)(2,1)} collective-permute-done((bf16[2400,800]{0,1:T(8,128)(2,1)}, bf16[2400,800]{0,1:T(8,128)(2,1)}, u32[]{:S(2)}, u32[]{:S(2)}) %collective-permute-start.1) | collective-permute-done | bytes 3840032 | tf_op jit(solution)/shard_map/ppermute | solution.py:23
  256.3 0.0 copy-start
  256.3 6.7 %pad_maximum_fusion.2 = bf16[4,1120,800]{1,2,0:T(8,128)(2,1)} fusion(bf16[1,2400,800]{1,2,0:T(8,128)(2,1)} %bitcast.4, bf16[1,2400,800]{1,2,0:T(8,128)(2,1)} %bitcast.16, bf16[1,2400,800]{1,2,0:T(8,128)(2,1)} %bitcast.2, bf16[1,2400,800]{1,2,0:T(8,128)(2,1)} %bitcast.1), kind=kLoop, calls=%fused_computation.6 | loop fusion | flops 28672000 | bytes 22528000 | tf_op jit(solution)/shard_map/gather | solution.py:32
  263.0 0.0 copy-done
  263.0 12.9 %pad_maximum_fusion.1 = bf16[4,2400,800]{1,2,0:T(8,128)(2,1)} fusion(bf16[1,2400,800]{1,2,0:T(8,128)(2,1)} %bitcast.4, bf16[1,2400,800]{1,2,0:T(8,128)(2,1)S(1)} %bitcast.17, bf16[1,2400,800]{1,2,0:T(8,128)(2,1)} %bitcast.2, bf16[1,2400,800]{1,2,0:T(8,128)(2,1)} %bitcast.1), kind=kLoop, calls=%fused_computation.5 | loop fusion | flops 23040000 | bytes 30720000 | tf_op jit(solution)/shard_map/stack | solution.py:28
  275.9 7.4 %gather_fusion = bf16[4,1120,800]{1,2,0:T(8,128)(2,1)} fusion(bf16[4,1120,800]{1,2,0:T(8,128)(2,1)} %pad_maximum_fusion.2, s32[1024]{0:T(1024)S(1)} %pad_clamp_fusion), kind=kCustom, calls=%fused_computation | custom fusion | bytes 14336016 | tf_op jit(solution)/shard_map/gather | solution.py:32
  283.3 11.2 %copy.15 = bf16[4,1120,800]{2,1,0:T(8,128)(2,1)} copy(bf16[4,1120,800]{1,2,0:T(8,128)(2,1)} %gather_fusion) | data formatting | bytes 14336000 | tf_op jit(solution)/shard_map/gather | solution.py:32
  294.4 7.0 %mini-gather-slice.2 = bf16[4,1280,800]{1,2,0:T(8,128)(2,1)} slice(bf16[4,2400,800]{1,2,0:T(8,128)(2,1)} %pad_maximum_fusion.1), slice={[0:4], [0:1280], [0:800]} | slice | bytes 16384000 | tf_op jit(solution)/shard_map/gather | solution.py:32
  301.5 37.2 %while.1 = (s32[]{:T(128)}, bf16[4,1280,800]{1,2,0:T(8,128)(2,1)}, s32[4,1]{0,1:T(1,128)S(1)}, bf16[4,1280,800]{2,1,0:T(8,128)(2,1)}, s32[]{:T(128)}) while((s32[]{:T(128)}, bf16[4,1280,800]{1,2,0:T(8,128)(2,1)}, s32[4,1]{0,1:T(1,128)S(1)}, bf16[4,1280,800]{2,1,0:T(8,128)(2,1)}, s32[]{:T(128)}) %tuple.17), condition=%wide.while_cond, body=%wide.while_body.sunk | while | flops 2 | bytes 12533849 | solution.py:32
  301.5 0.6 constant_dynamic-slice_fusion.4
  302.0 3.7 constant_dynamic-slice_fusion.5
  305.7 3.4 copy.18
  309.1 1.6 constant_dynamic-update-slice_fusion.2
  310.7 0.6 constant_dynamic-slice_fusion.4
  311.3 3.7 constant_dynamic-slice_fusion.5
  315.0 3.4 copy.18
  318.4 1.6 constant_dynamic-update-slice_fusion.2
  320.0 0.6 constant_dynamic-slice_fusion.4
  320.5 3.7 constant_dynamic-slice_fusion.5
  324.2 3.4 copy.18
  327.7 1.6 constant_dynamic-update-slice_fusion.2
  329.3 0.6 constant_dynamic-slice_fusion.4
  329.9 3.7 constant_dynamic-slice_fusion.5
  333.6 3.4 copy.18
  337.0 1.6 constant_dynamic-update-slice_fusion.2
  338.6 19.0 %pad_maximum_fusion = bf16[4,2400,800]{2,1,0:T(8,128)(2,1)} fusion(bf16[4,1120,800]{2,1,0:T(8,128)(2,1)} %copy.15, bf16[4,1280,800]{2,1,0:T(8,128)(2,1)} %get-tuple-element.12), kind=kLoop, calls=%fused_computation.4 | loop fusion | flops 30720000 | bytes 30720000
  357.6 8.3 %fusion.2 = f32[16,9600]{1,0:T(8,128)S(1)} fusion(bf16[16,800]{1,0:T(8,128)(2,1)S(1)} %select_n.40, bf16[9600,800]{1,0:T(8,128)(2,1)} %bitcast.15), kind=kOutput, calls=%fused_computation.16 | convolution fusion | flops 245760000 | bytes 16000000 | tf_op jit(solution)/shard_map/dot_general | solution.py:38
  365.8 28.9 %all-reduce.2 = bf16[16,9600]{1,0:T(8,128)(2,1)S(1)} all-reduce(f32[16,9600]{1,0:T(8,128)S(1)} %fusion.2), channel_id=2, replica_groups=mesh['row'=8,'col'=4] {'row'}, use_global_device_ids=true, to_apply=%region_0.1.clone | all-reduce | flops 153600 | bytes 921600
  394.7 0.7 dynamic-slice_convert_fusion
  (5 shorter events, 0.1 us)
Async XLA Ops:
  0.0 90.3 %collective-permute-start = (bf16[2400,800]{0,1:T(8,128)(2,1)}, bf16[2400,800]{0,1:T(8,128)(2,1)}, u32[]{:S(2)}, u32[]{:S(2)}) collective-permute-start(bf16[2400,800]{0,1:T(8,128)(2,1)} %param.5), channel_id=1, source_target_pairs={{0,1},{1,2},{2,3},{3,0},{4,5},{5,6},{6,7},{7,4},{8,9},{9,10},{10,1... | collective-permute-start | bytes 11520008 | tf_op jit(solution)/shard_map/ppermute | solution.py:23
  3.0 169.5 %collective-permute-start.2 = (bf16[2400,800]{0,1:T(8,128)(2,1)}, bf16[2400,800]{0,1:T(8,128)(2,1)}, u32[]{:S(2)}, u32[]{:S(2)}) collective-permute-start(bf16[2400,800]{0,1:T(8,128)(2,1)} %param.5), channel_id=1, source_target_pairs={{1,0},{2,1},{3,2},{0,3},{5,4},{6,5},{7,6},{4,7},{9,8},{10,9},{11,1... | collective-permute-start | bytes 11520008 | tf_op jit(solution)/shard_map/ppermute | solution.py:26
  90.3 165.9 %collective-permute-start.1 = (bf16[2400,800]{0,1:T(8,128)(2,1)}, bf16[2400,800]{0,1:T(8,128)(2,1)}, u32[]{:S(2)}, u32[]{:S(2)}) collective-permute-start(bf16[2400,800]{0,1:T(8,128)(2,1)} %collective-permute-done), channel_id=1, source_target_pairs={{0,1},{1,2},{2,3},{3,0},{4,5},{5,6},{6,7},{7,4},{8,9},{9,10},{10,1... | collective-permute-start | bytes 11520008 | tf_op jit(solution)/shard_map/ppermute | solution.py:23
  91.8 8.8 %all-to-all-start = ((bf16[2,8,800]{2,0,1:T(2,128)(2,1)}), bf16[2,8,800]{2,0,1:T(2,128)(2,1)S(1)}, u32[]{:S(2)}, u32[]{:S(2)}) async-start(bf16[2,8,800]{2,0,1:T(2,128)(2,1)} %copy.13), calls=%async_computation | async-start | bytes 57344 | tf_op jit(solution)/shard_map/all_to_all | solution.py:54
  256.3 6.7 %copy-start = (bf16[2400,800]{0,1:T(8,128)(2,1)S(1)}, bf16[2400,800]{0,1:T(8,128)(2,1)}, u32[]{:S(2)}) copy-start(bf16[2400,800]{0,1:T(8,128)(2,1)} %param.5) | copy-start | bytes 11520004

commit v2 on v0

--- a/solution.py
+++ b/solution.py
@@ -2,6 +2,18 @@
 import jax.numpy as jnp
 from jax import lax
 from jax.sharding import PartitionSpec as P
+
+
+def exchange_directly(array, axis, split, join):
+    ways, here = (lax.axis_size(axis), lax.axis_index(axis))
+    width = array.shape[split] // ways
+    turned = jnp.roll(array, -here * width, axis=split)
+    got = [lax.slice_in_dim(turned, 0, width, axis=split)]
+    for far in range(1, ways):
+        sent = lax.slice_in_dim(turned, far * width, (far + 1) * width, axis=split)
+        got.append(lax.ppermute(sent, axis, [(d, (d + far) % ways) for d in range(ways)]))
+    line = jnp.concatenate(got[::-1], axis=join)
+    return jnp.roll(line, (here + 1) * got[0].shape[join], axis=join)
 
 
 def contract(left, right):
@@ -21,7 +33,7 @@
 
 
 def body(amplitudes, panel, irrep_ij, irrep_ef):
-    blocked = lax.all_to_all(amplitudes, "row", split_axis=1, concat_axis=0, tiled=True)
+    blocked = exchange_directly(amplitudes, "row", 1, 0)
     allowed = ef_local(irrep_ij, irrep_ef, blocked)
     partial_terms = contract(allowed, lax.all_gather(panel, "col", axis=0, tiled=True))
     summed = lax.psum_scatter(partial_terms, "row", scatter_dimension=0, tiled=True)

time: 398 us -> 397 us (level)
    ppermute x0 -> x7, starting transfers between devices: none -> 8.32 us  [exchange_directly(): lax.ppermute(sent, axis, [(d, (d + far) % ways) for d in range(ways)])]
    all_to_all x1 -> x0, starting transfers between devices: 5.17 us -> none  [body(): lax.all_to_all(amplitudes, 'row', split_axis=1, concat_axis=0, tiled=True)]
  transfers between devices with their start and end apart: 2 -> 8, of which waited for: 2 -> 2; matrix products, arithmetic and copies ran while one was open for 1% -> 1% of each run, Pallas kernels for 0% -> 0%
where the time goes in v2:
time: 397 us
  waiting for transfers between devices  259 us (65%)
  local copies, waits for them, and re-layouts  76.5 us (19%)
  blocking collectives  31 us (8%)
  between operations  14.1 us (4%)
  starting transfers between devices  8.32 us (2%)
  matrix products  6.61 us (2%)
    all_gather x1, waiting for transfers between devices, body(): lax.all_gather(panel, 'col', axis=0, tiled=True)  258 us
    all_gather x1, local copies, waits for them, and re-layouts, body(): lax.all_gather(panel, 'col', axis=0, tiled=True)  48 us
    unnamed x1, blocking collectives  31 us
    unnamed x2, local copies, waits for them, and re-layouts  26.1 us
    ppermute x7, starting transfers between devices, exchange_directly(): lax.ppermute(sent, axis, [(d, (d + far) % ways) for d in range(ways)])  8.32 us
  transfers between devices with their start and end apart: 8, of which 2 were waited for; matrix products, arithmetic and copies ran while one was open for 1% of the time, Pallas kernels for 0%

profile of v2, /device:TPU:0, one launch (start us, length us, event | category | flops | bytes accessed | tf_op | source)
XLA Modules:
  0.0 396.6 jit_solution(7442310885666154230)
XLA Ops:
  6.5 0.0 all-gather.3.cloned.1.call-start
  6.5 0.7 all-gather.3.cloned.1.call-update
  7.3 0.9 fusion.4
  8.2 0.1 fusion.8
  8.3 3.4 collective-permute-start
  11.7 0.6 collective-permute-start.1
  12.4 0.2 collective-permute-start.2
  12.6 1.6 collective-permute-start.3
  14.2 0.1 collective-permute-start.4
  14.3 0.0 collective-permute-done
  14.3 2.3 collective-permute-start.5
  16.6 0.0 collective-permute-done.1
  16.6 0.0 collective-permute-start.6
  16.6 0.8 dynamic_slice.15
  17.4 0.7 dynamic_slice.14
  18.1 1.2 dynamic-slice
  20.0 0.0 collective-permute-done.2
  20.1 0.0 collective-permute-done.3
  20.1 0.0 collective-permute-done.4
  20.1 0.0 collective-permute-done.5
  20.1 0.5 collective-permute-done.6
  20.6 0.1 concatenate.11
  20.7 257.9 %all-gather.3.cloned.1.call-done = bf16[4,2400,800]{1,2,0:T(8,128)(2,1)} async-done(((bf16[1,2400,800]{1,2,0:T(8,128)(2,1)}), bf16[4,2400,800]{1,2,0:T(8,128)(2,1)}) %all-gather.3.cloned.1.call-update) | async-done | bytes 15360016 | tf_op jit(solution)/shard_map/all_gather | solution.py:38
  278.6 48.0 %copy.6 = bf16[4,2400,800]{1,0,2:T(4,128)(2,1)} copy(bf16[4,2400,800]{1,2,0:T(8,128)(2,1)} %all-gather.3.cloned.1.call-done) | data formatting | bytes 30720000 | tf_op jit(solution)/shard_map/all_gather | solution.py:38
  326.6 24.8 %reshape.3 = bf16[9600,800]{0,1:T(8,128)(2,1)} reshape(bf16[4,2400,800]{1,0,2:T(4,128)(2,1)} %copy.6) | data formatting | bytes 30720000
  351.5 6.6 %fusion = f32[16,9600]{1,0:T(8,128)S(1)} fusion(bf16[9600,800]{0,1:T(8,128)(2,1)} %reshape.3, bf16[32,800]{1,0:T(8,128)(2,1)S(1)} %concatenate.11, s32[]{:T(128)S(6)} %select_n.38, s32[800]{0:T(1024)S(1)} %dynamic_slice.15, s32[16]{0:T(128)S(1)} %dynamic_slice.14), kind=kOutput, calls=%fused_computation.4 | convolution fusion | flops 245785600 | bytes 16007684 | tf_op jit(solution)/shard_map/dot_general | solution.py:20
  358.1 31.0 %all-reduce.2 = bf16[16,9600]{1,0:T(8,128)(2,1)S(1)} all-reduce(f32[16,9600]{1,0:T(8,128)S(1)} %fusion), channel_id=2, replica_groups=mesh['row'=8,'col'=4] {'row'}, use_global_device_ids=true, to_apply=%region_0.1.clone | all-reduce | flops 153600 | bytes 921600
  389.1 0.7 dynamic-slice_convert_fusion
Async XLA Ops:
  6.5 272.1 %all-gather.3.cloned.1.call-start = ((), (), s32[]{:S(2)}) async-start(), calls=%async_computation | async-start | bytes 19456000 | tf_op jit(solution)/shard_map/all_gather | solution.py:38
  8.3 6.0 %collective-permute-start = (bf16[2,800]{1,0:T(2,128)(2,1)S(1)}, bf16[2,800]{1,0:T(2,128)(2,1)S(1)}, u32[]{:S(2)}, u32[]{:S(2)}) collective-permute-start(bf16[2,800]{1,0:T(2,128)(2,1)S(1)} %get-tuple-element.12), channel_id=1, source_target_pairs={{0,28},{4,0},{8,4},{12,8},{16,12},{20,16},{24,20},{28,24},{1,29},{... | collective-permute-start | bytes 9608 | tf_op jit(solution)/shard_map/ppermute | solution.py:14
  11.7 4.9 %collective-permute-start.1 = (bf16[2,800]{1,0:T(2,128)(2,1)S(1)}, bf16[2,800]{1,0:T(2,128)(2,1)S(1)}, u32[]{:S(2)}, u32[]{:S(2)}) collective-permute-start(bf16[2,800]{1,0:T(2,128)(2,1)S(1)} %get-tuple-element.11), channel_id=1, source_target_pairs={{0,24},{4,28},{8,0},{12,4},{16,8},{20,12},{24,16},{28,20},{1,25},{... | collective-permute-start | bytes 9608 | tf_op jit(solution)/shard_map/ppermute | solution.py:14
  12.4 7.7 %collective-permute-start.2 = (bf16[2,800]{1,0:T(2,128)(2,1)S(1)}, bf16[2,800]{1,0:T(2,128)(2,1)S(1)}, u32[]{:S(2)}, u32[]{:S(2)}) collective-permute-start(bf16[2,800]{1,0:T(2,128)(2,1)S(1)} %get-tuple-element.10), channel_id=1, source_target_pairs={{0,20},{4,24},{8,28},{12,0},{16,4},{20,8},{24,12},{28,16},{1,21},{... | collective-permute-start | bytes 9608 | tf_op jit(solution)/shard_map/ppermute | solution.py:14
  12.6 7.4 %collective-permute-start.3 = (bf16[2,800]{1,0:T(2,128)(2,1)S(1)}, bf16[2,800]{1,0:T(2,128)(2,1)S(1)}, u32[]{:S(2)}, u32[]{:S(2)}) collective-permute-start(bf16[2,800]{1,0:T(2,128)(2,1)S(1)} %get-tuple-element.9), channel_id=1, source_target_pairs={{0,16},{4,20},{8,24},{12,28},{16,0},{20,4},{24,8},{28,12},{1,17},{... | collective-permute-start | bytes 9608 | tf_op jit(solution)/shard_map/ppermute | solution.py:14
  14.2 5.9 %collective-permute-start.4 = (bf16[2,800]{1,0:T(2,128)(2,1)S(1)}, bf16[2,800]{1,0:T(2,128)(2,1)S(1)}, u32[]{:S(2)}, u32[]{:S(2)}) collective-permute-start(bf16[2,800]{1,0:T(2,128)(2,1)S(1)} %get-tuple-element.8), channel_id=1, source_target_pairs={{0,12},{4,16},{8,20},{12,24},{16,28},{20,0},{24,4},{28,8},{1,13},{... | collective-permute-start | bytes 9608 | tf_op jit(solution)/shard_map/ppermute | solution.py:14
  14.3 5.8 %collective-permute-start.5 = (bf16[2,800]{1,0:T(2,128)(2,1)S(1)}, bf16[2,800]{1,0:T(2,128)(2,1)S(1)}, u32[]{:S(2)}, u32[]{:S(2)}) collective-permute-start(bf16[2,800]{1,0:T(2,128)(2,1)S(1)} %get-tuple-element.7), channel_id=1, source_target_pairs={{0,8},{4,12},{8,16},{12,20},{16,24},{20,28},{24,0},{28,4},{1,9},{5... | collective-permute-start | bytes 9608 | tf_op jit(solution)/shard_map/ppermute | solution.py:14
  16.6 3.9 collective-permute-start.6
Sparse Core Ops, SparseCore 0:
  8.9 269.6 all-gather.2
